TPU v7x, 256 devices: a whole 4x4x8 slice. The times are simulated.
256 devices in a mesh: blk: 32 (over z, y_hi, core), head: 8 (over x, y_lo).
Axes of the slice: x: 4, y: 4 (y_hi: 2, y_lo: 2; y = y_hi * 2 + y_lo), z: 8, core: 2. Of those that a mesh axis runs over, the one named last changes fastest.
Arguments:
- frames: bfloat16 [32768, 2048], P(('blk', 'head')), may hold values from -20.4 to 20.4
- qkv_weight: bfloat16 [2048, 6144], P(None, 'head'), may hold values from -0.125 to 0.125
- out_weight: bfloat16 [2048, 2048], P('head'), may hold values from -0.125 to 0.125
- recording: int32 [32768], P(('blk', 'head')), may hold values from 0 to 63, never falling along the last dimension, each value on 1 to 1024 neighbouring positions
Outputs:
- encoded: bfloat16 [32768, 2048], P(('blk', 'head'))
Inputs may be any that keep to these rules, and one draw needn't show every extreme that they name: Recording ids never fall along the frames; each recording holds 1 to 1024 frames, and one holds exactly 1024.
All inputs are finite; a program needn't handle non-finite values.
Results may differ from a plain program's by a relative error of at most 0.019.
The roundings to bfloat16 on the way count: a program that leaves them out, or rounds other values in their place, can miss the bound.
Values may be sent and summed in bfloat16 or wider, within the bound.
A program may use at most 64 MiB of HBM per device.

v0:
```python
import functools

import jax
import jax.numpy as jnp
from jax import lax
from jax.experimental import pallas as pl
from jax.experimental.pallas import tpu as pltpu
from jax.sharding import PartitionSpec as P

HEAD_DIM = 128
MESH = pl.DeviceIdType.MESH
NX, NZ, NB = 4, 8, 32
BF = jnp.bfloat16
F32 = jnp.float32
NEG = -jnp.inf


def mod(a, n):
    return lax.rem(a + 2 * n, n)


def kernel(
    frames, qw_in, ow, ids, out,
    F, QW, W, Q, KV, H, RL, IDS, HID, RID, QID, ATS, ATR, ACC, M, L, A,
    loc, ag_s, ag_r, id_s, id_r, hid_s, hid_r, sib_s, sib_r, off_s, off_r, rel_s, rel_r,
    wp_s, wp_r, wx_s, wx_r, wu_s, wu_r, wd_s, wd_r, ws_s, ws_r, at_s, at_r,
):
    blk = lax.axis_index("blk")
    head = lax.axis_index("head")
    z = blk // 4
    yh = lax.rem(blk, 4) // 2
    c = lax.rem(blk, 2)
    x = head // 2
    yl = lax.rem(head, 2)

    def block(dx, f):
        return mod(x + dx, NX) * 2 + lax.rem(yl + f, 2)

    def peer(dx, f):
        return (blk, block(dx, f))

    right, left, across = peer(1, 0), peer(-1, 0), peer(0, 1)
    sibling = (blk + 1 - 2 * c, head)
    lean = 1 - 2 * yh
    ahead = (mod(blk + 4 * lean, NB), head)
    behind = (mod(blk - 4 * lean, NB), head)
    owner_blk = z * 4 + (1 - yh) * 2 + c
    owner_head = x * 2 + 1 - yl
    relay = (owner_blk, owner_head)
    relay_to = (mod(owner_blk + 2 * c - 1, NB), owner_head)
    far = mod(blk + 2 * c - 1, NB)
    relay_from = ((far // 4) * 4 + (1 - lax.rem(far, 4) // 2) * 2 + lax.rem(far, 2), owner_head)
    base_off = 8 * (1 - c)
    base_sib = 8 * c

    def remote(src, dst, ss, rs, dev):
        return pltpu.make_async_remote_copy(
            src_ref=src, dst_ref=dst, send_sem=ss, recv_sem=rs, device_id=dev, device_id_type=MESH
        )

    load_qw = pltpu.make_async_copy(qw_in, QW, loc.at[0])
    load_own = pltpu.make_async_copy(frames, F.at[head], loc.at[1])
    load_w = pltpu.make_async_copy(ow, W.at[0], loc.at[2])
    load_own.start()
    load_qw.start()
    load_w.start()
    rels = [(dx, f) for f in range(2) for dx in range(NX)]
    partners = [peer(dx, f) for dx, f in rels[1:]]
    partners += [sibling, ahead, behind, relay, relay_to, relay_from, (far, head)]
    barrier = pltpu.get_barrier_semaphore()
    for p in partners:
        pl.semaphore_signal(barrier, inc=1, device_id=p, device_id_type=MESH)
    pl.semaphore_wait(barrier, len(partners))

    idc = [None]
    for k in range(1, 8):
        dx, f = rels[k]
        back = f * NX + (-dx) % NX
        idc.append(remote(ids, IDS.at[head], id_s.at[k], id_r.at[back], peer(dx, f)))
        idc[k].start()
    IDS[head] = ids[...]

    def w_piece(dx, s, i):
        zs = mod(z + s * lean, NZ)
        back = (-dx) % NX
        return remote(ow.at[zs, c], W.at[back, zs, c], wp_s.at[5 * dx + i], wp_r.at[5 * back + i], peer(dx, 0))

    def w_piece_wait(dx, s, i):
        ref = W.at[dx, mod(z + s * lean, NZ), c]
        remote(ref, ref, wp_s.at[5 * dx + i], wp_r.at[5 * dx + i], right).wait_recv()

    for dx in (1, 3, 2):
        w_piece(dx, 0, 0).start()

    def fr(dx, f, start, rows=64):
        return F.at[block(dx, f), pl.ds(start, rows)]

    def gather_copy(i, src, dst, dev):
        return remote(src, dst, ag_s.at[i], ag_r.at[i], dev)

    plan = {
        "A0": ((0, 0, 0), right, (-1, 0, 0)),
        "B1": ((0, 0, 64), left, (1, 0, 64)),
        "C0": ((0, 0, 0), across, (0, 1, 0)),
        "A1": ((0, 0, 64), right, (-1, 0, 64)),
        "B0": ((0, 0, 0), left, (1, 0, 0)),
        "C1": ((0, 0, 64), across, (0, 1, 64)),
        "F0": ((0, 1, 0), right, (-1, 1, 0)),
        "G0": ((0, 1, 32, 32), left, (1, 1, 32, 32)),
        "F1": ((0, 1, 64, 32), right, (-1, 1, 64, 32)),
        "G1": ((0, 1, 64), left, (1, 1, 64)),
        "J": ((-1, 0, 96, 32), across, (-1, 1, 96, 32)),
        "K": ((1, 0, 0, 32), across, (1, 1, 0, 32)),
        "D": ((-1, 0, 0), right, (2, 0, 0)),
        "E": ((1, 0, 64), left, (2, 0, 64)),
        "H": ((-1, 1, 0), right, (2, 1, 0)),
        "I": ((1, 1, 64), left, (2, 1, 64)),
    }
    send, recv = {}, {}
    for i, (name, (what, to, comes)) in enumerate(plan.items()):
        src = frames.at[pl.ds(what[2], 64)] if what[:2] == (0, 0) else fr(*what)
        send[name] = gather_copy(i, src, fr(*what), to)
        recv[name] = gather_copy(i, fr(*comes), fr(*comes), to)
    send["C0"].start()

    def sib_copy(b):
        return remote(KV.at[b], H.at[base_sib + b], sib_s.at[b], sib_r.at[b], sibling)

    def off_copy(b):
        return remote(KV.at[b], RL.at[b], off_s.at[b], off_r.at[b], relay)

    def direct_copy(b):
        return remote(KV.at[b], H.at[base_off + b], off_s.at[b], rel_r.at[b], (far, head))

    def relay_copy(b):
        return remote(RL.at[b], H.at[base_off + b], rel_s.at[b], rel_r.at[b], relay_to)

    def project(b, direct=False):
        r = jnp.dot(F[b], QW[...], preferred_element_type=F32).astype(BF)
        for hd in range(2):
            o = hd * 3 * HEAD_DIM
            cols = pl.ds(hd * HEAD_DIM, HEAD_DIM)
            Q[b, :, cols] = r[:, o : o + HEAD_DIM]
            KV[b, 0, :, cols] = r[:, o + HEAD_DIM : o + 2 * HEAD_DIM]
            KV[b, 1, :, cols] = r[:, o + 2 * HEAD_DIM : o + 3 * HEAD_DIM]
        (direct_copy(b) if direct else off_copy(b)).start()
        sib_copy(b).start()

    def pass_on(dx, f):
        b = mod(x + dx, NX) * 2 + lax.rem(1 - yl + f, 2)
        remote(RL.at[b], RL.at[b], off_s.at[b], off_r.at[b], relay).wait_recv()
        relay_copy(b).start()

    PART = ((1, 3), (4, 4))
    STEPS = {(0, True): 1, (0, False): 2, (1, True): 3, (1, False): 4}

    def w_set(s, part, core):
        return W.at[pl.ds(*PART[part]), mod(z + s * lean, NZ), core]

    def w_copy(ref, s, part, leaning):
        i = part * 5 + s
        if leaning:
            return remote(ref, ref, wu_s.at[i], wu_r.at[i], ahead)
        return remote(ref, ref, wd_s.at[i], wd_r.at[i], behind)

    def w_send(s, part, leaning):
        return w_copy(w_set((1 - s) if leaning else (s - 1), part, c), s, part, leaning)

    def w_recv(s, part, leaning):
        return w_copy(w_set(-s if leaning else s, part, c), s, part, leaning)

    def w_sib(j, part):
        ref = w_set(j, part, c)
        return remote(ref, ref, ws_s.at[part * 8 + j], ws_r.at[part * 8 + j], sibling)

    def w_sib_recv(j, part):
        ref = w_set(j, part, 1 - c)
        return remote(ref, ref, ws_s.at[part * 8 + j], ws_r.at[part * 8 + j], sibling)

    def w_first(part):
        w_send(1, part, True).start()
        w_send(1, part, False).start()
        w_sib(0, part).start()

    def w_step(s, part, leaning):
        w_recv(s, part, leaning).wait_recv()
        if s < STEPS[part, leaning]:
            w_send(s + 1, part, leaning).start()
        w_sib(8 - s if leaning else s, part).start()

    w_swap = remote(W.at[pl.ds(0, 4), z, c], W.at[pl.ds(4, 4), z, c], wx_s.at[0], wx_r.at[0], relay)

    load_own.wait()
    load_qw.wait()
    for dx in (1, 3, 2):
        w_piece(dx, 0, 0).wait_send()
    for name in ("A0", "B1", "A1", "B0", "C1"):
        send[name].start()
    project(head)
    load_w.wait()
    for dx in (1, 3, 2):
        w_piece_wait(dx, 0, 0)
    w_swap.start()
    w_first(0)

    for k in range(1, 8):
        dx, f = rels[k]
        row = IDS.at[block(dx, f)]
        remote(row, row, id_s.at[k], id_r.at[k], across).wait_recv()
    ids_sib = remote(IDS, HID.at[pl.ds(base_sib, 8)], hid_s.at[0], hid_r.at[0], sibling)
    ids_off = remote(IDS, RID, hid_s.at[1], hid_r.at[1], relay)
    ids_rel = remote(RID, HID.at[pl.ds(base_off, 8)], hid_s.at[2], hid_r.at[2], relay_to)
    ids_off.start()
    ids_sib.start()
    for b in range(8):
        QID[b] = jnp.transpose(jnp.broadcast_to(IDS[b], (128, 128)))

    scale = HEAD_DIM ** (-0.5)
    dims = (((1,), (1,)), ((), ()))

    def attend(dx, chunks, first, last):
        a = mod(x + dx, NX)
        q_at = pl.ds(2 * a, 2)
        qid = QID[q_at].reshape(256, 128)
        kid = jnp.concatenate([r[b + j] for _, r, b in chunks for j in range(2)], axis=1)
        mask = jnp.concatenate([qid] * (2 * len(chunks)), axis=1) == kid
        for hd in range(2):
            cols = pl.ds(hd * HEAD_DIM, HEAD_DIM)
            q = Q[q_at, :, cols].reshape(256, HEAD_DIM)
            k, v = (
                jnp.concatenate([r[pl.ds(b, 2), n, :, cols].reshape(256, HEAD_DIM) for r, _, b in chunks], axis=0)
                for n in range(2)
            )
            s = lax.dot_general(q, k, dims, preferred_element_type=F32) * scale
            s = jnp.where(mask, s, NEG)
            m = jnp.max(s, axis=1, keepdims=True)
            if not first:
                m0 = M[a, hd]
                m = jnp.maximum(m0, m)
                decay = jnp.exp(m0 - m)
            p = jnp.exp(s - m)
            total = jnp.sum(p, axis=1, keepdims=True)
            mixed = jnp.dot(p.astype(BF), v, preferred_element_type=F32)
            if not first:
                total = L[a, hd] * decay + total
                mixed = A[a, hd] * decay + mixed
            if last:
                mixed = (mixed / total).astype(BF)
                for f in range(2):
                    rel = lax.rem(yl + f, 2) * NX + dx
                    ATS[rel, :, cols] = mixed[128 * f : 128 * (f + 1)]
            else:
                M[a, hd] = m
                L[a, hd] = total
                A[a, hd] = mixed

    def own(dx):
        return (KV, IDS, 2 * mod(x + dx, NX))

    def halo(dx, side):
        return (H, HID, 8 * side + 2 * mod(x + dx, NX))

    def facing(dx, key_dx):
        side = jnp.where(mod(x + key_dx, NX) >= mod(x + dx, NX), 0, 1)
        return halo(key_dx, side)

    near = (0, 1, -1)

    def each_near(body):
        def step(t, carry):
            body(lax.rem(3 + t, NX))
            return carry

        lax.fori_loop(0, 3, step, 0)

    def halo_wait(dx, f):
        b = block(dx, f)
        hs, ho = H.at[8 - base_sib + b], H.at[8 - base_off + b]
        remote(hs, hs, sib_s.at[b], sib_r.at[b], sibling).wait_recv()
        remote(ho, ho, rel_s.at[b], rel_r.at[b], sibling).wait_recv()

    pass_on(0, 0)
    w_step(1, 0, False)
    w_step(1, 0, True)
    w_swap.wait_recv()
    w_first(1)
    recv["C0"].wait_recv()
    send["F0"].start()
    send["G0"].start()
    recv["C1"].wait_recv()
    send["F1"].start()
    send["G1"].start()
    project(block(0, 1))
    recv["A0"].wait_recv()
    recv["A1"].wait_recv()
    send["J"].start()
    recv["B1"].wait_recv()
    recv["B0"].wait_recv()
    send["K"].start()
    project(block(-1, 0))
    project(block(1, 0))
    w_step(1, 1, True)
    w_step(2, 0, False)
    w_step(1, 1, False)
    pass_on(0, 1)
    ids_off.wait_recv()
    ids_rel.start()
    send["F1"].wait_send()
    send["D"].start()
    send["G1"].wait_send()
    send["E"].start()
    recv["F0"].wait_recv()
    send["H"].start()
    recv["G1"].wait_recv()
    send["I"].start()
    recv["G0"].wait_recv()
    recv["K"].wait_recv()
    project(block(1, 1))
    recv["F1"].wait_recv()
    recv["J"].wait_recv()
    project(block(-1, 1))
    pass_on(-1, 0)
    pass_on(1, 0)
    w_step(2, 1, True)
    attend(0, [own(n) for n in near], True, False)
    attend(1, [own(n) for n in near], True, False)
    w_step(2, 1, False)
    attend(3, [own(n) for n in near], True, False)
    pass_on(1, 1)
    pass_on(-1, 1)
    for name in ("D", "E", "H", "I"):
        send[name].wait_send()
    for i in range(4):
        for dx in (1, 3, 2):
            w_piece(dx, 3 + i, 1 + i).start()
    recv["D"].wait_recv()
    recv["E"].wait_recv()
    project(block(2, 0))
    recv["H"].wait_recv()
    recv["I"].wait_recv()
    project(block(2, 1), direct=True)
    w_step(3, 1, False)
    w_step(3, 1, True)
    pass_on(2, 0)

    hs, ho = HID.at[pl.ds(8 - base_sib, 8)], HID.at[pl.ds(8 - base_off, 8)]
    remote(hs, hs, hid_s.at[0], hid_r.at[0], sibling).wait_recv()
    remote(ho, ho, hid_s.at[2], hid_r.at[2], sibling).wait_recv()
    for dx in near:
        for f in range(2):
            halo_wait(dx, f)
    attend(2, [own(n) for n in near] + [own(2)] + [facing(2, n) for n in near], True, False)
    w_step(4, 1, False)
    each_near(lambda dx: attend(dx, [own(2)] + [facing(dx, n) for n in near] + [halo(dx, 1)], False, False))
    for i in range(4):
        for dx in (1, 3, 2):
            w_piece_wait(dx, 3 + i, 1 + i)
        w_sib(3 + i, 0).start()
    halo_wait(2, 0)
    halo_wait(2, 1)

    def hand_over(dx):
        for f in range(2):
            rel = f * NX + dx
            back = f * NX + mod(-dx, NX)

            @pl.when(rel > 0)
            def _():
                remote(ATS.at[rel], ATR.at[back], at_s.at[rel], at_r.at[back], peer(dx, f)).start()

    def finish(dx, chunks):
        attend(dx, chunks, False, True)
        hand_over(dx)

    finish(2, [halo(2, 0), halo(2, 1)])
    each_near(lambda dx: finish(dx, [facing(dx, 2)]))

    for j in range(8):
        w_sib_recv(j, 0).wait_recv()
        w_sib_recv(j, 1).wait_recv()

    def out_part(a, d):
        return jnp.dot(a, W[d].reshape(256, 2048), preferred_element_type=F32)

    ACC[...] = out_part(ATS[0], 0)

    def out_step(t, carry):
        d = lax.rem(2 + 4 * t, 7) + jnp.where(lax.rem(2 + 4 * t, 7) == 0, 7, 0)
        remote(ATR.at[d], ATR.at[d], at_s.at[d], at_r.at[d], sibling).wait_recv()
        ACC[...] += out_part(ATR[d], d)
        return carry

    lax.fori_loop(0, 7, out_step, 0)
    out[...] = ACC[...].astype(BF)

    for k in range(1, 8):
        idc[k].wait_send()
        remote(ATS.at[k], ATR.at[k], at_s.at[k], at_r.at[k], sibling).wait_send()
    for name in plan:
        if name not in ("F1", "G1", "D", "E", "H", "I"):
            send[name].wait_send()
    for i in range(4):
        for dx in (1, 3, 2):
            w_piece(dx, 3 + i, 1 + i).wait_send()
    w_swap.wait_send()
    for b in range(8):
        sib_copy(b).wait_send()
        off_copy(b).wait_send()
        w_sib(b, 0).wait_send()
        w_sib(b, 1).wait_send()
    for k in range(7):
        dx, f = ((0, 0), (0, 1), (-1, 0), (1, 0), (-1, 1), (1, 1), (2, 0))[k]
        relay_copy(mod(x + dx, NX) * 2 + lax.rem(1 - yl + f, 2)).wait_send()
    ids_sib.wait_send()
    ids_off.wait_send()
    ids_rel.wait_send()
    for (part, leaning), n in STEPS.items():
        for s in range(1, n + 1):
            w_send(s, part, leaning).wait_send()


def shards(frames, qkv_weight, out_weight, recording):
    dma = pltpu.SemaphoreType.DMA
    any_ = pl.BlockSpec(memory_space=pl.ANY)
    vmem = pl.BlockSpec(memory_space=pltpu.VMEM)
    V = pltpu.VMEM
    return pl.pallas_call(
        kernel,
        name="encoder_block",
        out_shape=jax.ShapeDtypeStruct((128, 2048), BF),
        in_specs=[any_, any_, any_, vmem],
        out_specs=vmem,
        scratch_shapes=[
            V((8, 128, 2048), BF),
            V((2048, 768), BF),
            V((8, 8, 2, 16, 2048), BF),
            V((8, 128, 256), BF),
            V((8, 2, 128, 256), BF),
            V((16, 2, 128, 256), BF),
            V((8, 2, 128, 256), BF),
            V((8, 1, 128), jnp.int32),
            V((16, 1, 128), jnp.int32),
            V((8, 1, 128), jnp.int32),
            V((8, 128, 128), jnp.int32),
            V((8, 128, 256), BF),
            V((8, 128, 256), BF),
            V((128, 2048), F32),
            V((4, 2, 256, 1), F32),
            V((4, 2, 256, 1), F32),
            V((4, 2, 256, 128), F32),
            dma((3,)),
            dma((16,)), dma((16,)),
            dma((8,)), dma((8,)),
            dma((3,)), dma((3,)),
            dma((8,)), dma((8,)),
            dma((8,)), dma((8,)),
            dma((8,)), dma((8,)),
            dma((20,)), dma((20,)),
            dma((1,)), dma((1,)),
            dma((10,)), dma((10,)),
            dma((10,)), dma((10,)),
            dma((16,)), dma((16,)),
            dma((8,)), dma((8,)),
        ],
        compiler_params=pltpu.CompilerParams(
            collective_id=0, has_side_effects=True, vmem_limit_bytes=56 * 2**20
        ),
    )(frames, qkv_weight, out_weight.reshape(8, 2, 16, 2048), recording.reshape(1, 128))


def solution(mesh):
    in_specs = (P(("blk", "head"), None), P(None, "head"), P("head", None), P(("blk", "head")))
    out_specs = P(("blk", "head"), None)
    return jax.shard_map(shards, mesh=mesh, in_specs=in_specs, out_specs=out_specs, check_vma=False)
```

profile of v0, /device:TPU:1, one launch (start us, length us, event | category | flops | bytes accessed | tf_op | source)
XLA Modules:
  0.0 77.4 jit_solution(17301955945883292718)
XLA Ops:
  0.0 75.5 %encoder_block.1 = bf16[128,2048]{1,0:T(8,128)(2,1)} custom-call(bf16[128,2048]{1,0:T(8,128)(2,1)} %frames.1, bf16[2048,768]{1,0:T(8,128)(2,1)} %qw_in.1, bf16[8,2,16,2048]{3,2,1,0:T(8,128)(2,1)} %bitcast.2, s32[1,128]{1,0:T(1,128)} %bitcast.3), custom_call_target="tpu_custom_call" | custom-call | tf_op jit(solution)/shard_map/encoder_block/pallas_call | solution.py:427
  75.6 1.9 %copy.6 = bf16[128,2048]{1,0:T(8,128)(2,1)} copy(bf16[128,2048]{1,0:T(8,128)(2,1)} %encoder_block.1) | data formatting | bytes 1048576
where the time goes:
time: 77.6 us; the launch traced here: 77.4 us
  Pallas kernels  75.5 us (97%)
  local copies, waits for them, and re-layouts  1.88 us (2%)
    pallas_call x1, Pallas kernels, shards(): pl.pallas_call(kernel, name='encoder_block', out_shape=jax.ShapeDtypeStru...  75.5 us
    unnamed x1, local copies, waits for them, and re-layouts  1.88 us

commit v1 on v0

--- a/solution.py
+++ b/solution.py
@@ -91,6 +91,8 @@
 
     for dx in (1, 3, 2):
         w_piece(dx, 0, 0).start()
+    w_own = remote(ow.at[z, c], W.at[4, z, c], wx_s.at[1], wx_r.at[1], relay)
+    w_own.start()
 
     def fr(dx, f, start, rows=64):
         return F.at[block(dx, f), pl.ds(start, rows)]
@@ -152,7 +154,7 @@
         relay_copy(b).start()
 
     PART = ((1, 3), (4, 4))
-    STEPS = {(0, True): 1, (0, False): 2, (1, True): 3, (1, False): 4}
+    STEPS = {(0, True): 1, (0, False): 3, (1, True): 3, (1, False): 4}
 
     def w_set(s, part, core):
         return W.at[pl.ds(*PART[part]), mod(z + s * lean, NZ), core]
@@ -188,7 +190,7 @@
             w_send(s + 1, part, leaning).start()
         w_sib(8 - s if leaning else s, part).start()
 
-    w_swap = remote(W.at[pl.ds(0, 4), z, c], W.at[pl.ds(4, 4), z, c], wx_s.at[0], wx_r.at[0], relay)
+    w_swap = remote(W.at[pl.ds(1, 3), z, c], W.at[pl.ds(5, 3), z, c], wx_s.at[0], wx_r.at[0], relay)
 
     load_own.wait()
     load_qw.wait()
@@ -196,24 +198,12 @@
         w_piece(dx, 0, 0).wait_send()
     for name in ("A0", "B1", "A1", "B0", "C1"):
         send[name].start()
-    project(head)
     load_w.wait()
     for dx in (1, 3, 2):
         w_piece_wait(dx, 0, 0)
     w_swap.start()
     w_first(0)
-
-    for k in range(1, 8):
-        dx, f = rels[k]
-        row = IDS.at[block(dx, f)]
-        remote(row, row, id_s.at[k], id_r.at[k], across).wait_recv()
-    ids_sib = remote(IDS, HID.at[pl.ds(base_sib, 8)], hid_s.at[0], hid_r.at[0], sibling)
-    ids_off = remote(IDS, RID, hid_s.at[1], hid_r.at[1], relay)
-    ids_rel = remote(RID, HID.at[pl.ds(base_off, 8)], hid_s.at[2], hid_r.at[2], relay_to)
-    ids_off.start()
-    ids_sib.start()
-    for b in range(8):
-        QID[b] = jnp.transpose(jnp.broadcast_to(IDS[b], (128, 128)))
+    project(head)
 
     scale = HEAD_DIM ** (-0.5)
     dims = (((1,), (1,)), ((), ()))
@@ -279,9 +269,17 @@
         remote(hs, hs, sib_s.at[b], sib_r.at[b], sibling).wait_recv()
         remote(ho, ho, rel_s.at[b], rel_r.at[b], sibling).wait_recv()
 
-    pass_on(0, 0)
+    def near_halo_wait(dx):
+        if dx == 0:
+            hs, ho = HID.at[pl.ds(8 - base_sib, 8)], HID.at[pl.ds(8 - base_off, 8)]
+            remote(hs, hs, hid_s.at[0], hid_r.at[0], sibling).wait_recv()
+            remote(ho, ho, hid_s.at[2], hid_r.at[2], sibling).wait_recv()
+        halo_wait(dx, 0)
+        halo_wait(dx, 1)
+
     w_step(1, 0, False)
     w_step(1, 0, True)
+    w_own.wait_recv()
     w_swap.wait_recv()
     w_first(1)
     recv["C0"].wait_recv()
@@ -290,6 +288,18 @@
     recv["C1"].wait_recv()
     send["F1"].start()
     send["G1"].start()
+    pass_on(0, 0)
+    for k in range(1, 8):
+        dx, f = rels[k]
+        row = IDS.at[block(dx, f)]
+        remote(row, row, id_s.at[k], id_r.at[k], across).wait_recv()
+    ids_sib = remote(IDS, HID.at[pl.ds(base_sib, 8)], hid_s.at[0], hid_r.at[0], sibling)
+    ids_off = remote(IDS, RID, hid_s.at[1], hid_r.at[1], relay)
+    ids_rel = remote(RID, HID.at[pl.ds(base_off, 8)], hid_s.at[2], hid_r.at[2], relay_to)
+    ids_off.start()
+    ids_sib.start()
+    for b in range(8):
+        QID[b] = jnp.transpose(jnp.broadcast_to(IDS[b], (128, 128)))
     project(block(0, 1))
     recv["A0"].wait_recv()
     recv["A1"].wait_recv()
@@ -322,40 +332,36 @@
     pass_on(-1, 0)
     pass_on(1, 0)
     w_step(2, 1, True)
-    attend(0, [own(n) for n in near], True, False)
-    attend(1, [own(n) for n in near], True, False)
+    near_halo_wait(0)
+    each_near(lambda dx: attend(dx, [own(n) for n in near] + [facing(dx, 0)], True, False))
     w_step(2, 1, False)
-    attend(3, [own(n) for n in near], True, False)
+    w_step(3, 0, False)
     pass_on(1, 1)
     pass_on(-1, 1)
     for name in ("D", "E", "H", "I"):
         send[name].wait_send()
-    for i in range(4):
+    for i in range(3):
         for dx in (1, 3, 2):
-            w_piece(dx, 3 + i, 1 + i).start()
+            w_piece(dx, 4 + i, 1 + i).start()
     recv["D"].wait_recv()
     recv["E"].wait_recv()
     project(block(2, 0))
     recv["H"].wait_recv()
     recv["I"].wait_recv()
     project(block(2, 1), direct=True)
+    attend(2, [own(n) for n in near] + [own(2)], True, False)
+    pass_on(2, 0)
     w_step(3, 1, False)
+    near_halo_wait(1)
+    near_halo_wait(-1)
+    each_near(lambda dx: attend(dx, [own(2), facing(dx, 1), facing(dx, -1), halo(dx, 1)], False, False))
     w_step(3, 1, True)
-    pass_on(2, 0)
-
-    hs, ho = HID.at[pl.ds(8 - base_sib, 8)], HID.at[pl.ds(8 - base_off, 8)]
-    remote(hs, hs, hid_s.at[0], hid_r.at[0], sibling).wait_recv()
-    remote(ho, ho, hid_s.at[2], hid_r.at[2], sibling).wait_recv()
-    for dx in near:
-        for f in range(2):
-            halo_wait(dx, f)
-    attend(2, [own(n) for n in near] + [own(2)] + [facing(2, n) for n in near], True, False)
+    attend(2, [facing(2, n) for n in near], False, False)
     w_step(4, 1, False)
-    each_near(lambda dx: attend(dx, [own(2)] + [facing(dx, n) for n in near] + [halo(dx, 1)], False, False))
-    for i in range(4):
+    for i in range(3):
         for dx in (1, 3, 2):
-            w_piece_wait(dx, 3 + i, 1 + i)
-        w_sib(3 + i, 0).start()
+            w_piece_wait(dx, 4 + i, 1 + i)
+        w_sib(4 + i, 0).start()
     halo_wait(2, 0)
     halo_wait(2, 1)
 
@@ -399,9 +405,10 @@
     for name in plan:
         if name not in ("F1", "G1", "D", "E", "H", "I"):
             send[name].wait_send()
-    for i in range(4):
+    for i in range(3):
         for dx in (1, 3, 2):
-            w_piece(dx, 3 + i, 1 + i).wait_send()
+            w_piece(dx, 4 + i, 1 + i).wait_send()
+    w_own.wait_send()
     w_swap.wait_send()
     for b in range(8):
         sib_copy(b).wait_send()
@@ -456,7 +463,7 @@
             dma((8,)), dma((8,)),
             dma((8,)), dma((8,)),
             dma((20,)), dma((20,)),
-            dma((1,)), dma((1,)),
+            dma((2,)), dma((2,)),
             dma((10,)), dma((10,)),
             dma((10,)), dma((10,)),
             dma((16,)), dma((16,)),

time: 77.6 us -> 74.9 us (0.965)
  Pallas kernels: 75.5 us -> 72.4 us
    pallas_call x1, Pallas kernels: 75.5 us -> 72.4 us  [shards(): pl.pallas_call(kernel, name='encoder_block', out_shape=jax.ShapeDtypeStru...]
where the time goes in v1:
time: 74.9 us; the launch traced here: 74.3 us
  Pallas kernels  72.4 us (97%)
  local copies, waits for them, and re-layouts  1.88 us (3%)
    pallas_call x1, Pallas kernels, shards(): pl.pallas_call(kernel, name='encoder_block', out_shape=jax.ShapeDtypeStru...  72.4 us
    unnamed x1, local copies, waits for them, and re-layouts  1.88 us

profile of v1, /device:TPU:1, one launch (start us, length us, event | category | flops | bytes accessed | tf_op | source)
XLA Modules:
  0.0 74.3 jit_solution(13689562371029901681)
XLA Ops:
  0.0 72.4 %encoder_block.1 = bf16[128,2048]{1,0:T(8,128)(2,1)} custom-call(bf16[128,2048]{1,0:T(8,128)(2,1)} %frames.1, bf16[2048,768]{1,0:T(8,128)(2,1)} %qw_in.1, bf16[8,2,16,2048]{3,2,1,0:T(8,128)(2,1)} %bitcast.2, s32[1,128]{1,0:T(1,128)} %bitcast.3), custom_call_target="tpu_custom_call" | custom-call | tf_op jit(solution)/shard_map/encoder_block/pallas_call | solution.py:434
  72.5 1.9 %copy.6 = bf16[128,2048]{1,0:T(8,128)(2,1)} copy(bf16[128,2048]{1,0:T(8,128)(2,1)} %encoder_block.1) | data formatting | bytes 1048576

commit v2 on v1

--- a/solution.py
+++ b/solution.py
@@ -256,9 +256,11 @@
 
     near = (0, 1, -1)
 
-    def each_near(body):
+    def each_near(body, then=()):
         def step(t, carry):
             body(lax.rem(3 + t, NX))
+            for n, event in enumerate(then):
+                pl.when(t == n)(event)
             return carry
 
         lax.fori_loop(0, 3, step, 0)
@@ -333,10 +335,16 @@
     pass_on(1, 0)
     w_step(2, 1, True)
     near_halo_wait(0)
-    each_near(lambda dx: attend(dx, [own(n) for n in near] + [facing(dx, 0)], True, False))
-    w_step(2, 1, False)
-    w_step(3, 0, False)
-    pass_on(1, 1)
+    def between_0():
+        w_step(2, 1, False)
+
+    def between_1():
+        w_step(3, 0, False)
+        pass_on(1, 1)
+
+    each_near(
+        lambda dx: attend(dx, [own(n) for n in near] + [facing(dx, 0)], True, False), (between_0, between_1)
+    )
     pass_on(-1, 1)
     for name in ("D", "E", "H", "I"):
         send[name].wait_send()

time: 74.9 us -> 74.6 us (level)
  no operation moved by 1% of the time
where the time goes in v2:
time: 74.6 us; the launch traced here: 74.5 us
  Pallas kernels  72.6 us (97%)
  local copies, waits for them, and re-layouts  1.88 us (3%)
    pallas_call x1, Pallas kernels, shards(): pl.pallas_call(kernel, name='encoder_block', out_shape=jax.ShapeDtypeStru...  72.6 us
    unnamed x1, local copies, waits for them, and re-layouts  1.88 us

profile of v2, /device:TPU:1, one launch (start us, length us, event | category | flops | bytes accessed | tf_op | source)
XLA Modules:
  0.0 74.5 jit_solution(1492992874496027363)
XLA Ops:
  0.0 72.6 %encoder_block.1 = bf16[128,2048]{1,0:T(8,128)(2,1)} custom-call(bf16[128,2048]{1,0:T(8,128)(2,1)} %frames.1, bf16[2048,768]{1,0:T(8,128)(2,1)} %qw_in.1, bf16[8,2,16,2048]{3,2,1,0:T(8,128)(2,1)} %bitcast.2, s32[1,128]{1,0:T(1,128)} %bitcast.3), custom_call_target="tpu_custom_call" | custom-call | tf_op jit(solution)/shard_map/encoder_block/pallas_call | solution.py:442
  72.6 1.9 %copy.6 = bf16[128,2048]{1,0:T(8,128)(2,1)} copy(bf16[128,2048]{1,0:T(8,128)(2,1)} %encoder_block.1) | data formatting | bytes 1048576

commit v3 on v2

--- a/solution.py
+++ b/solution.py
@@ -309,8 +309,7 @@
     recv["B1"].wait_recv()
     recv["B0"].wait_recv()
     send["K"].start()
-    project(block(-1, 0))
-    project(block(1, 0))
+    lax.fori_loop(0, 2, lambda t, carry: (project(block(3 - 2 * t, 0)), carry)[1], 0)
     w_step(1, 1, True)
     w_step(2, 0, False)
     w_step(1, 1, False)
@@ -396,15 +395,21 @@
     def out_part(a, d):
         return jnp.dot(a, W[d].reshape(256, 2048), preferred_element_type=F32)
 
-    ACC[...] = out_part(ATS[0], 0)
+    ACC[...] = jnp.zeros_like(ACC)
+    ATR[0] = ATS[0]
 
     def out_step(t, carry):
-        d = lax.rem(2 + 4 * t, 7) + jnp.where(lax.rem(2 + 4 * t, 7) == 0, 7, 0)
-        remote(ATR.at[d], ATR.at[d], at_s.at[d], at_r.at[d], sibling).wait_recv()
+        turn = lax.rem(4 * t + 5, 7)
+        d = jnp.where(t == 0, 0, jnp.where(turn == 0, 7, turn))
+
+        @pl.when(t > 0)
+        def _():
+            remote(ATR.at[d], ATR.at[d], at_s.at[d], at_r.at[d], sibling).wait_recv()
+
         ACC[...] += out_part(ATR[d], d)
         return carry
 
-    lax.fori_loop(0, 7, out_step, 0)
+    lax.fori_loop(0, 8, out_step, 0)
     out[...] = ACC[...].astype(BF)
 
     for k in range(1, 8):

time: 74.6 us -> 74.8 us (level)
  no operation moved by 1% of the time
where the time goes in v3:
time: 74.8 us; the launch traced here: 74.7 us
  Pallas kernels  72.8 us (97%)
  local copies, waits for them, and re-layouts  1.88 us (3%)
    pallas_call x1, Pallas kernels, shards(): pl.pallas_call(kernel, name='encoder_block', out_shape=jax.ShapeDtypeStru...  72.8 us
    unnamed x1, local copies, waits for them, and re-layouts  1.88 us

profile of v3, /device:TPU:1, one launch (start us, length us, event | category | flops | bytes accessed | tf_op | source)
XLA Modules:
  0.0 74.7 jit_solution(11720757856961455854)
XLA Ops:
  0.0 72.8 %encoder_block.1 = bf16[128,2048]{1,0:T(8,128)(2,1)} custom-call(bf16[128,2048]{1,0:T(8,128)(2,1)} %frames.1, bf16[2048,768]{1,0:T(8,128)(2,1)} %qw_in.1, bf16[8,2,16,2048]{3,2,1,0:T(8,128)(2,1)} %bitcast.2, s32[1,128]{1,0:T(1,128)} %bitcast.3), custom_call_target="tpu_custom_call" | custom-call | tf_op jit(solution)/shard_map/encoder_block/pallas_call | solution.py:447
  72.8 1.9 %copy.6 = bf16[128,2048]{1,0:T(8,128)(2,1)} copy(bf16[128,2048]{1,0:T(8,128)(2,1)} %encoder_block.1) | data formatting | bytes 1048576
